TPU v7x, 32 devices: a whole 2x2x4 slice. The times are simulated.
32 devices in a mesh: sys: 2 (over x), row: 4 (over y, core), col: 4 (over z).
Axes of the slice: x: 2, y: 2, z: 4, core: 2. Of those that a mesh axis runs over, the one named last changes fastest.
Arguments:
- density: bfloat16 [4, 4, 8, 19, 128, 128], P('row', 'col', 'sys'), parts along dimension 2, may hold values from -0.5 to 0.5, as said below
- neighbours: int32 [4, 4, 8, 19], P('row', 'col', 'sys'), parts along dimension 2, may hold values from -1 to 63, as said below
- square_pattern: int32 [4, 4, 4, 50], P('row', 'col', 'sys'), parts along dimension 2, may hold values from -1 to 63, as said below
Outputs:
- purified: bfloat16 [4, 4, 4, 19, 128, 128], P('row', 'col', 'sys'), parts along dimension 2
There are 2 independent parts, one for each index of `sys`. A program takes and returns all parts, laid end to end along the dimension named above; each array names one. Nothing has to cross between parts.
Inputs may be any that keep to these rules, and one draw needn't show every extreme that they name: `density`: block w of row g holds the block of P at (g, neighbours[g, w]); the block at (j, g) is the transpose of the one at (g, j), and slots whose neighbour is -1 hold zeros. `neighbours`: row g of the whole array lists, in any order and each once, the groups j whose block P[g, j] is stored, g itself always among them, with -1 in the unused slots; j is listed in row g exactly when g is listed in row j. Group g belongs to the device at row index g // 16 and col index (g // 4) % 4, as its plane g % 4; every listed group belongs to that same device or to one of the eight devices next to it along row, col or both, and a listed group of a device that differs along both row and col has the same plane as g. `square_pattern`: row l of a device lists, in any order and each once, with -1 in the unused slots, groups m for which some group k is listed in the neighbours row of that device's plane l + 1 and m is listed in the neighbours row of k: the blocks of the square kept after filtering, all of them where there are at most 50.
All inputs are finite; a program needn't handle non-finite values.
Results may differ from a plain program's by a relative error of at most 0.0038.
Values may be sent and summed in bfloat16 or wider, within the bound.
A program may use at most 128 MiB of HBM per device.

v0:
```python
import jax
import jax.numpy as jnp
from jax import lax
from jax.sharding import PartitionSpec as P


def extended(block, sides, width):
    for axis, dim in sides:
        count = lax.axis_size(axis)
        forward = [(i, i + 1) for i in range(count - 1)]
        backward = [(target, source) for source, target in forward]
        low = lax.ppermute(
            lax.slice_in_dim(block, block.shape[dim] - width, None, axis=dim), axis, forward
        )
        high = lax.ppermute(lax.slice_in_dim(block, 0, width, axis=dim), axis, backward)
        block = jnp.concatenate([low, block, high], axis=dim)
    return block


def shortened(shard):
    return jax.tree.map(lambda a: a.astype(jnp.bfloat16) if a.dtype == jnp.float32 else a, shard)


def find_slots(wanted, listed):
    slot_count = listed.shape[-1]
    matches = (wanted[..., None] == listed) & (wanted[..., None] >= 0)
    places = jnp.sum(jnp.where(matches, jnp.arange(slot_count, dtype=jnp.int32), 0), axis=-1)
    return jnp.where(jnp.any(matches, axis=-1), places, slot_count)


def shards(density, neighbours, square_pattern):
    plane_count, slot_count, block_size = (density.shape[2], density.shape[3], density.shape[4])
    square_slots = square_pattern.shape[3]
    side_blocks, side_cols = (
        extended(density, (("col", 1),), 1),
        extended(neighbours, (("col", 1),), 1),
    )
    near_blocks, near_cols = (
        extended(side_blocks, (("row", 0),), 1),
        extended(shortened(side_cols), (("row", 0),), 1).astype(side_cols.dtype),
    )
    flat_blocks = near_blocks.reshape(9 * plane_count, slot_count, block_size, block_size)
    flat_cols = near_cols.reshape(9 * plane_count, slot_count)
    col_total = lax.axis_size("col")
    row_here = lax.axis_index("row")
    col_here = lax.axis_index("col")

    def held_at(groups):
        clamped = jnp.maximum(groups, 0)
        cell_index = clamped // plane_count
        row_step = cell_index // col_total - row_here + 1
        col_step = cell_index % col_total - col_here + 1
        position = (row_step * 3 + col_step) * plane_count + clamped % plane_count
        return jnp.where(groups >= 0, position, 4 * plane_count)

    def one_row(inputs):
        own_blocks, own_cols, list_two = inputs
        present = own_cols >= 0
        spots = held_at(own_cols)
        near_rows = flat_blocks[spots]
        row_cols = flat_cols[spots]
        both_live = present[:, None] & (row_cols >= 0)
        target = jnp.where(both_live, find_slots(row_cols, list_two), square_slots)
        summed = jnp.zeros((square_slots + 1, block_size, block_size), jnp.float32)
        for start_slot in range(0, slot_count, 5):
            products = jnp.einsum(
                "kab,kwbc->kwac",
                own_blocks[start_slot : start_slot + 5],
                near_rows[start_slot : start_slot + 5],
                preferred_element_type=jnp.float32,
            )
            summed = summed + jax.ops.segment_sum(
                products.reshape(-1, block_size, block_size),
                target[start_slot : start_slot + 5].reshape(-1),
                num_segments=square_slots + 1,
            )
        square = summed[:square_slots].astype(jnp.bfloat16)
        padded = jnp.concatenate(
            [square, jnp.zeros((1, block_size, block_size), jnp.bfloat16)], axis=0
        )
        chosen = jnp.where(row_cols >= 0, find_slots(row_cols, list_two), square_slots)
        cubed = jnp.einsum(
            "jwab,jwcb->jac", padded[chosen], near_rows, preferred_element_type=jnp.float32
        )
        own_place = jnp.where(present, find_slots(own_cols, list_two), square_slots)
        updated = 3.0 * padded[own_place].astype(jnp.float32) - 2.0 * cubed
        return jnp.where(present[:, None, None], updated, 0.0).astype(jnp.bfloat16)

    purified = lax.map(
        one_row,
        (
            density[0, 0, 1 : plane_count - 1],
            neighbours[0, 0, 1 : plane_count - 1],
            square_pattern[0, 0],
        ),
    )
    return purified[None, None]


def solution(mesh):
    in_specs = (
        P("row", "col", "sys", None, None, None),
        P("row", "col", "sys", None),
        P("row", "col", "sys", None),
    )
    out_specs = P("row", "col", "sys", None, None, None)
    return jax.shard_map(shards, mesh=mesh, in_specs=in_specs, out_specs=out_specs, check_vma=False)
```

profile of v0, /device:TPU:11, one launch (start us, length us, event | category | flops | bytes accessed | tf_op | source)
XLA Modules:
  0.0 480.1 jit_solution(10777517012098421733)
XLA Ops:
  0.0 3.3 collective-permute-start.4
  3.3 2.2 collective-permute-start.5
  5.6 51.6 %collective-permute-done.4 = bf16[1,1,4,19,128,128]{5,4,3,2,1,0:T(8,128)(2,1)S(1)} collective-permute-done((bf16[1,1,4,19,128,128]{5,4,3,2,1,0:T(8,128)(2,1)}, bf16[1,1,4,19,128,128]{5,4,3,2,1,0:T(8,128)(2,1)S(1)}, u32[]{:S(2)}, u32[]{:S(2)}) %collective-permute-start.4) | collective-permute-done | bytes 2490400 | tf_op jit(solution)/shard_map/ppermute | solution.py:12
  62.4 4.6 collective-permute-start.6
  67.0 3.1 collective-permute-start.7
  70.1 3.2 collective-permute-start
  75.6 2.1 collective-permute-done.1
  77.7 3.8 collective-permute-start.2
  83.5 64.3 %collective-permute-done.2 = s32[1,3,4,19]{3,2,1,0:T(4,128)S(1)} collective-permute-done((s32[1,3,4,19]{3,2,1,0:T(4,128)S(1)}, s32[1,3,4,19]{3,2,1,0:T(4,128)S(1)}, u32[]{:S(2)}, u32[]{:S(2)}) %collective-permute-start.2) | collective-permute-done | bytes 944 | tf_op jit(solution)/shard_map/ppermute | solution.py:12
  147.8 4.4 collective-permute-done.3
  152.3 15.9 %pad_maximum_fusion = bf16[3,3,4,19,128,128]{5,4,3,2,1,0:T(8,128)(2,1)} fusion(bf16[1,3,4,19,128,128]{5,4,3,2,1,0:T(8,128)(2,1)} %collective-permute-done.7, bf16[1,3,4,19,128,128]{5,4,3,2,1,0:T(8,128)(2,1)} %constant_dynamic-update-slice_fusion.3, bf16[1,3,4,19,128,128]{5,4,3,2,1,0:T(8,128)(2,1)} %collective-permute-done.6), kind=kLoop, calls=%fused_computation.63 | loop fusion | flops 22413312 | bytes 44826624 | tf_op jit(solution)/shard_map/concatenate | solution.py:16
  168.2 312.0 %while.13 = (s32[]{:T(128)}, bf16[2,19,128,128]{3,2,1,0:T(8,128)(2,1)}, s32[2,19]{1,0:T(2,128)S(1)}, s32[]{:T(128)}, s32[]{:T(128)}, /*index=5*/s32[36,19]{1,0:T...) while((s32[]{:T(128)}, ...), condition=%wide.region_9.10_spmd, body=%wide.region_0.9_spmd.sunk | while | flops 3039552512 | bytes 341885408 | solution.py:89
  168.6 13.3 %gather_fusion.1 = bf16[19,19,128,128]{3,2,1,0:T(8,128)(2,1)} fusion(bf16[36,19,128,128]{3,2,1,0:T(8,128)(2,1)} %get-tuple-element.291, s32[1024]{0:T(1024)S(1)} %get-tuple-element.247), kind=kCustom, calls=%fused_computation.1.clone.1 | custom fusion | bytes 23658572 | tf_op jit(solution)/shard_map/while/body/eval_jaxpr/gather | solution.py:60
  182.0 5.6 %fusion.59 = f32[5,19,128,128]{3,2,1,0:T(8,128)} fusion(bf16[19,19,128,128]{3,2,1,0:T(8,128)(2,1)} %gather_fusion.1, bf16[2,19,128,128]{3,2,1,0:T(8,128)(2,1)S(1)} %get-tuple-element.292, s32[]{:T(128)} %get-tuple-element.268, s32[]{:T(128)S(6)} %add.253), kind=kOutput, calls=%fused_computation.22.clone.1 | convolution fusion | flops 398458880 | bytes 18219016 | tf_op jit(solution)/shard_map/while/body/eval_jaxpr/kab,kwbc->kwac/dot_general | solution.py:66
  187.6 6.5 %copy.35 = f32[95,128,128]{2,1,0:T(8,128)} copy(f32[95,128,128]{1,2,0:T(8,128)} %bitcast.162) | data formatting | bytes 12451840 | tf_op jit(solution)/shard_map/while/body/eval_jaxpr/reshape | solution.py:73
  196.4 12.9 %scatter_fusion.1 = f32[51,128,128]{2,1,0:T(8,128)S(1)} fusion(f32[51,128,128]{2,1,0:T(8,128)S(1)} %broadcast.632.clone.1, s32[95]{0:T(128)S(1)} %reshape.492, f32[95,128,128]{2,1,0:T(8,128)} %copy.35), kind=kCustom, calls=%fused_computation.5.clone.1 | custom fusion | flops 1556480 | bytes 18678140 | tf_op jit(solution)/shard_map/while/body/eval_jaxpr/scatter-add | solution.py:72
  209.3 6.8 %fusion.58 = f32[5,19,128,128]{3,2,1,0:T(8,128)} fusion(bf16[19,19,128,128]{3,2,1,0:T(8,128)(2,1)} %gather_fusion.1, bf16[2,19,128,128]{3,2,1,0:T(8,128)(2,1)} %copy-done.3, s32[]{:T(128)} %get-tuple-element.268), kind=kOutput, calls=%fused_computation.24.clone.1 | convolution fusion | flops 398458880 | bytes 18219520 | tf_op jit(solution)/shard_map/while/body/eval_jaxpr/kab,kwbc->kwac/dot_general | solution.py:66
  216.1 6.5 %copy.34 = f32[95,128,128]{2,1,0:T(8,128)} copy(f32[95,128,128]{1,2,0:T(8,128)} %bitcast.161) | data formatting | bytes 12451840 | tf_op jit(solution)/shard_map/while/body/eval_jaxpr/reshape | solution.py:73
  222.7 2.1 broadcast.632.clone
  224.8 19.7 %scatter_fusion = f32[51,128,128]{2,1,0:T(8,128)} fusion(f32[51,128,128]{2,1,0:T(8,128)} %broadcast.632.clone, s32[95]{0:T(128)S(1)} %reshape.491, f32[95,128,128]{2,1,0:T(8,128)} %copy.34), kind=kCustom, calls=%fused_computation.4.clone.1 | custom fusion | flops 1556480 | bytes 18678140 | tf_op jit(solution)/shard_map/while/body/eval_jaxpr/scatter-add | solution.py:72
  244.5 3.5 add.254
  248.0 5.6 %fusion.60 = f32[5,19,128,128]{3,2,1,0:T(8,128)} fusion(bf16[19,19,128,128]{3,2,1,0:T(8,128)(2,1)} %gather_fusion.1, bf16[2,19,128,128]{3,2,1,0:T(8,128)(2,1)} %copy-done.3, s32[]{:T(128)} %get-tuple-element.268, s32[]{:T(128)S(6)} %add.255), kind=kOutput, calls=%fused_computation.20.clone.1 | convolution fusion | flops 398458880 | bytes 18219524 | tf_op jit(solution)/shard_map/while/body/eval_jaxpr/kab,kwbc->kwac/dot_general | solution.py:66
  253.7 6.5 %copy.36 = f32[95,128,128]{2,1,0:T(8,128)} copy(f32[95,128,128]{1,2,0:T(8,128)} %bitcast.163) | data formatting | bytes 12451840 | tf_op jit(solution)/shard_map/while/body/eval_jaxpr/reshape | solution.py:73
  260.3 12.9 %scatter_fusion.2 = f32[51,128,128]{2,1,0:T(8,128)S(1)} fusion(f32[51,128,128]{2,1,0:T(8,128)S(1)} %add.254, s32[95]{0:T(128)S(1)} %reshape.493, f32[95,128,128]{2,1,0:T(8,128)} %copy.36), kind=kCustom, calls=%fused_computation.6.clone.1 | custom fusion | flops 1556480 | bytes 18678140 | tf_op jit(solution)/shard_map/while/body/eval_jaxpr/scatter-add | solution.py:72
  273.2 6.2 %fusion.61 = f32[4,19,128,128]{3,2,1,0:T(8,128)} fusion(bf16[19,19,128,128]{3,2,1,0:T(8,128)(2,1)} %gather_fusion.1, bf16[2,19,128,128]{3,2,1,0:T(8,128)(2,1)} %copy-done.3, s32[]{:T(128)} %get-tuple-element.268, s32[]{:T(128)S(6)} %add.256), kind=kOutput, calls=%fused_computation.26.clone.1 | convolution fusion | flops 318767104 | bytes 16941572 | tf_op jit(solution)/shard_map/while/body/eval_jaxpr/kab,kwbc->kwac/dot_general | solution.py:66
  279.4 5.8 %copy.37 = f32[76,128,128]{2,1,0:T(8,128)} copy(f32[76,128,128]{1,2,0:T(8,128)} %bitcast.164) | data formatting | bytes 9961472 | tf_op jit(solution)/shard_map/while/body/eval_jaxpr/reshape | solution.py:73
  285.7 10.8 %scatter_fusion.3 = f32[51,128,128]{2,1,0:T(8,128)S(1)} fusion(f32[51,128,128]{2,1,0:T(8,128)S(1)} %broadcast.632.clone.2, s32[76]{0:T(128)S(1)} %reshape.494, f32[76,128,128]{2,1,0:T(8,128)} %copy.37), kind=kCustom, calls=%fused_computation.7.clone.1 | custom fusion | flops 1245184 | bytes 14942512 | tf_op jit(solution)/shard_map/while/body/eval_jaxpr/scatter-add | solution.py:72
  298.2 3.4 fusion.62
  301.7 10.9 %gather_fusion.2 = bf16[361,128,128]{2,1,0:T(8,128)(2,1)} fusion(bf16[51,128,128]{2,1,0:T(8,128)(2,1)S(1)} %fusion.62, s32[1024]{0:T(1024)S(1)} %pad_clamp_fusion.6), kind=kCustom, calls=%fused_computation.3.clone.1 | custom fusion | bytes 23659940 | tf_op jit(solution)/shard_map/while/body/eval_jaxpr/gather | solution.py:83
  313.4 10.7 %fusion.63 = bf16[2,19,128,128]{3,2,1,0:T(8,128)(2,1)} fusion(bf16[2,19,128,128]{3,2,1,0:T(8,128)(2,1)} %get-tuple-element.269, s32[]{:T(128)} %get-tuple-element.268, bf16[19,19,128,128]{3,2,1,0:T(8,128)(2,1)} %bitcast.166, bf16[19,19,128,128]{3,2,1,0:T(8,128)(2,1)} %gather_fusion.1, bf16[19,128,128]{2,1,0:T(8,128)(2,1)S(1)} %gather_fusion.3, ...), kind=kOutput, calls=%fused_computation.15.clone.1 | convolution fusion | flops 1516011520 | bytes 24904212 | tf_op jit(solution)/shard_map/while/body/eval_jaxpr/jwab,jwcb->jac/dot_general | solution.py:82
  324.6 13.3 %gather_fusion.1 = bf16[19,19,128,128]{3,2,1,0:T(8,128)(2,1)} fusion(bf16[36,19,128,128]{3,2,1,0:T(8,128)(2,1)} %get-tuple-element.291, s32[1024]{0:T(1024)S(1)} %get-tuple-element.247), kind=kCustom, calls=%fused_computation.1.clone.1 | custom fusion | bytes 23658572 | tf_op jit(solution)/shard_map/while/body/eval_jaxpr/gather | solution.py:60
  337.9 5.6 %fusion.59 = f32[5,19,128,128]{3,2,1,0:T(8,128)} fusion(bf16[19,19,128,128]{3,2,1,0:T(8,128)(2,1)} %gather_fusion.1, bf16[2,19,128,128]{3,2,1,0:T(8,128)(2,1)S(1)} %get-tuple-element.292, s32[]{:T(128)} %get-tuple-element.268, s32[]{:T(128)S(6)} %add.253), kind=kOutput, calls=%fused_computation.22.clone.1 | convolution fusion | flops 398458880 | bytes 18219016 | tf_op jit(solution)/shard_map/while/body/eval_jaxpr/kab,kwbc->kwac/dot_general | solution.py:66
  343.5 6.5 %copy.35 = f32[95,128,128]{2,1,0:T(8,128)} copy(f32[95,128,128]{1,2,0:T(8,128)} %bitcast.162) | data formatting | bytes 12451840 | tf_op jit(solution)/shard_map/while/body/eval_jaxpr/reshape | solution.py:73
  352.3 12.9 %scatter_fusion.1 = f32[51,128,128]{2,1,0:T(8,128)S(1)} fusion(f32[51,128,128]{2,1,0:T(8,128)S(1)} %broadcast.632.clone.1, s32[95]{0:T(128)S(1)} %reshape.492, f32[95,128,128]{2,1,0:T(8,128)} %copy.35), kind=kCustom, calls=%fused_computation.5.clone.1 | custom fusion | flops 1556480 | bytes 18678140 | tf_op jit(solution)/shard_map/while/body/eval_jaxpr/scatter-add | solution.py:72
  365.2 6.8 %fusion.58 = f32[5,19,128,128]{3,2,1,0:T(8,128)} fusion(bf16[19,19,128,128]{3,2,1,0:T(8,128)(2,1)} %gather_fusion.1, bf16[2,19,128,128]{3,2,1,0:T(8,128)(2,1)} %copy-done.3, s32[]{:T(128)} %get-tuple-element.268), kind=kOutput, calls=%fused_computation.24.clone.1 | convolution fusion | flops 398458880 | bytes 18219520 | tf_op jit(solution)/shard_map/while/body/eval_jaxpr/kab,kwbc->kwac/dot_general | solution.py:66
  372.1 6.5 %copy.34 = f32[95,128,128]{2,1,0:T(8,128)} copy(f32[95,128,128]{1,2,0:T(8,128)} %bitcast.161) | data formatting | bytes 12451840 | tf_op jit(solution)/shard_map/while/body/eval_jaxpr/reshape | solution.py:73
  378.7 2.1 broadcast.632.clone
  380.8 19.8 %scatter_fusion = f32[51,128,128]{2,1,0:T(8,128)} fusion(f32[51,128,128]{2,1,0:T(8,128)} %broadcast.632.clone, s32[95]{0:T(128)S(1)} %reshape.491, f32[95,128,128]{2,1,0:T(8,128)} %copy.34), kind=kCustom, calls=%fused_computation.4.clone.1 | custom fusion | flops 1556480 | bytes 18678140 | tf_op jit(solution)/shard_map/while/body/eval_jaxpr/scatter-add | solution.py:72
  400.5 3.5 add.254
  404.1 5.6 %fusion.60 = f32[5,19,128,128]{3,2,1,0:T(8,128)} fusion(bf16[19,19,128,128]{3,2,1,0:T(8,128)(2,1)} %gather_fusion.1, bf16[2,19,128,128]{3,2,1,0:T(8,128)(2,1)} %copy-done.3, s32[]{:T(128)} %get-tuple-element.268, s32[]{:T(128)S(6)} %add.255), kind=kOutput, calls=%fused_computation.20.clone.1 | convolution fusion | flops 398458880 | bytes 18219524 | tf_op jit(solution)/shard_map/while/body/eval_jaxpr/kab,kwbc->kwac/dot_general | solution.py:66
  409.7 6.5 %copy.36 = f32[95,128,128]{2,1,0:T(8,128)} copy(f32[95,128,128]{1,2,0:T(8,128)} %bitcast.163) | data formatting | bytes 12451840 | tf_op jit(solution)/shard_map/while/body/eval_jaxpr/reshape | solution.py:73
  416.3 12.9 %scatter_fusion.2 = f32[51,128,128]{2,1,0:T(8,128)S(1)} fusion(f32[51,128,128]{2,1,0:T(8,128)S(1)} %add.254, s32[95]{0:T(128)S(1)} %reshape.493, f32[95,128,128]{2,1,0:T(8,128)} %copy.36), kind=kCustom, calls=%fused_computation.6.clone.1 | custom fusion | flops 1556480 | bytes 18678140 | tf_op jit(solution)/shard_map/while/body/eval_jaxpr/scatter-add | solution.py:72
  429.2 6.2 %fusion.61 = f32[4,19,128,128]{3,2,1,0:T(8,128)} fusion(bf16[19,19,128,128]{3,2,1,0:T(8,128)(2,1)} %gather_fusion.1, bf16[2,19,128,128]{3,2,1,0:T(8,128)(2,1)} %copy-done.3, s32[]{:T(128)} %get-tuple-element.268, s32[]{:T(128)S(6)} %add.256), kind=kOutput, calls=%fused_computation.26.clone.1 | convolution fusion | flops 318767104 | bytes 16941572 | tf_op jit(solution)/shard_map/while/body/eval_jaxpr/kab,kwbc->kwac/dot_general | solution.py:66
  435.4 5.8 %copy.37 = f32[76,128,128]{2,1,0:T(8,128)} copy(f32[76,128,128]{1,2,0:T(8,128)} %bitcast.164) | data formatting | bytes 9961472 | tf_op jit(solution)/shard_map/while/body/eval_jaxpr/reshape | solution.py:73
  441.7 10.8 %scatter_fusion.3 = f32[51,128,128]{2,1,0:T(8,128)S(1)} fusion(f32[51,128,128]{2,1,0:T(8,128)S(1)} %broadcast.632.clone.2, s32[76]{0:T(128)S(1)} %reshape.494, f32[76,128,128]{2,1,0:T(8,128)} %copy.37), kind=kCustom, calls=%fused_computation.7.clone.1 | custom fusion | flops 1245184 | bytes 14942512 | tf_op jit(solution)/shard_map/while/body/eval_jaxpr/scatter-add | solution.py:72
  454.2 3.4 fusion.62
  457.7 11.0 %gather_fusion.2 = bf16[361,128,128]{2,1,0:T(8,128)(2,1)} fusion(bf16[51,128,128]{2,1,0:T(8,128)(2,1)S(1)} %fusion.62, s32[1024]{0:T(1024)S(1)} %pad_clamp_fusion.6), kind=kCustom, calls=%fused_computation.3.clone.1 | custom fusion | bytes 23659940 | tf_op jit(solution)/shard_map/while/body/eval_jaxpr/gather | solution.py:83
  469.4 10.7 %fusion.63 = bf16[2,19,128,128]{3,2,1,0:T(8,128)(2,1)} fusion(bf16[2,19,128,128]{3,2,1,0:T(8,128)(2,1)} %get-tuple-element.269, s32[]{:T(128)} %get-tuple-element.268, bf16[19,19,128,128]{3,2,1,0:T(8,128)(2,1)} %bitcast.166, bf16[19,19,128,128]{3,2,1,0:T(8,128)(2,1)} %gather_fusion.1, bf16[19,128,128]{2,1,0:T(8,128)(2,1)S(1)} %gather_fusion.3, ...), kind=kOutput, calls=%fused_computation.15.clone.1 | convolution fusion | flops 1516011520 | bytes 24904212 | tf_op jit(solution)/shard_map/while/body/eval_jaxpr/jwab,jwcb->jac/dot_general | solution.py:82
  (91 shorter events, 21.1 us)
Async XLA Ops:
  0.0 58.9 %copy-start.5 = (bf16[1,1,4,19,128,128]{5,4,3,2,1,0:T(8,128)(2,1)S(1)}, bf16[1,1,4,19,128,128]{5,4,3,2,1,0:T(8,128)(2,1)}, u32[]{:S(2)}) copy-start(bf16[1,1,4,19,128,128]{5,4,3,2,1,0:T(8,128)(2,1)} %param.5) | copy-start | bytes 7471108
  0.0 70.1 %copy-start.7 = (s32[1,1,4,19]{3,2,1,0:T(4,128)S(1)}, s32[1,1,4,19]{3,2,1,0:T(4,128)}, u32[]{:S(2)}) copy-start(s32[1,1,4,19]{3,2,1,0:T(4,128)} %param.6) | copy-start | bytes 916
  0.0 57.1 %collective-permute-start.4 = (bf16[1,1,4,19,128,128]{5,4,3,2,1,0:T(8,128)(2,1)}, bf16[1,1,4,19,128,128]{5,4,3,2,1,0:T(8,128)(2,1)S(1)}, u32[]{:S(2)}, u32[]{:S(2)}) collective-permute-start(bf16[1,1,4,19,128,128]{5,4,3,2,1,0:T(8,128)(2,1)} %param.5), channel_id=1, source_target_pairs={{0,1},{1,2},{2,3},{4,5},{5,6},{6,7},{8,9},{9,10},{10,11},{12,13},{... | collective-permute-start | bytes 7471112 | tf_op jit(solution)/shard_map/ppermute | solution.py:12
  3.3 57.3 %collective-permute-start.5 = (bf16[1,1,4,19,128,128]{5,4,3,2,1,0:T(8,128)(2,1)}, bf16[1,1,4,19,128,128]{5,4,3,2,1,0:T(8,128)(2,1)S(1)}, u32[]{:S(2)}, u32[]{:S(2)}) collective-permute-start(bf16[1,1,4,19,128,128]{5,4,3,2,1,0:T(8,128)(2,1)} %param.5), channel_id=1, source_target_pairs={{1,0},{2,1},{3,2},{5,4},{6,5},{7,6},{9,8},{10,9},{11,10},{13,12},{... | collective-permute-start | bytes 7471112 | tf_op jit(solution)/shard_map/ppermute | solution.py:15
  62.4 89.9 %collective-permute-start.6 = (bf16[1,3,4,19,128,128]{5,4,3,2,1,0:T(8,128)(2,1)}, bf16[1,3,4,19,128,128]{5,4,3,2,1,0:T(8,128)(2,1)}, u32[]{:S(2)}, u32[]{:S(2)}) collective-permute-start(bf16[1,3,4,19,128,128]{5,4,3,2,1,0:T(8,128)(2,1)} %constant_dynamic-update-slice_fusion.3), channel_id=1, source_target_pairs={{0,4},{4,8},{8,12},{1,5},{5,9},{9,13},{2,6},{6,10},{10,14},{3,7},{... | collective-permute-start | bytes 22413320 | tf_op jit(solution)/shard_map/ppermute | solution.py:12
  67.0 85.3 %collective-permute-start.7 = (bf16[1,3,4,19,128,128]{5,4,3,2,1,0:T(8,128)(2,1)}, bf16[1,3,4,19,128,128]{5,4,3,2,1,0:T(8,128)(2,1)}, u32[]{:S(2)}, u32[]{:S(2)}) collective-permute-start(bf16[1,3,4,19,128,128]{5,4,3,2,1,0:T(8,128)(2,1)} %constant_dynamic-update-slice_fusion.3), channel_id=1, source_target_pairs={{4,0},{8,4},{12,8},{5,1},{9,5},{13,9},{6,2},{10,6},{14,10},{7,3},{... | collective-permute-start | bytes 22413320 | tf_op jit(solution)/shard_map/ppermute | solution.py:15
  70.1 5.4 %collective-permute-start = (s32[1,1,4,19]{3,2,1,0:T(4,128)S(1)}, s32[1,1,4,19]{3,2,1,0:T(4,128)S(1)}, u32[]{:S(2)}, u32[]{:S(2)}) collective-permute-start(s32[1,1,4,19]{3,2,1,0:T(4,128)S(1)} %copy-done.7), channel_id=1, source_target_pairs={{0,1},{1,2},{2,3},{4,5},{5,6},{6,7},{8,9},{9,10},{10,11},{12,13},{... | collective-permute-start | bytes 920 | tf_op jit(solution)/shard_map/ppermute | solution.py:12
  73.3 4.3 collective-permute-start.1
  77.7 70.1 %collective-permute-start.2 = (s32[1,3,4,19]{3,2,1,0:T(4,128)S(1)}, s32[1,3,4,19]{3,2,1,0:T(4,128)S(1)}, u32[]{:S(2)}, u32[]{:S(2)}) collective-permute-start(s32[1,3,4,19]{3,2,1,0:T(4,128)S(1)} %constant_dynamic-update-slice_fusion), channel_id=1, source_target_pairs={{0,4},{4,8},{8,12},{1,5},{5,9},{9,13},{2,6},{6,10},{10,14},{3,7},{... | collective-permute-start | bytes 2744 | tf_op jit(solution)/shard_map/ppermute | solution.py:12
  81.5 70.7 %collective-permute-start.3 = (s32[1,3,4,19]{3,2,1,0:T(4,128)S(1)}, s32[1,3,4,19]{3,2,1,0:T(4,128)S(1)}, u32[]{:S(2)}, u32[]{:S(2)}) collective-permute-start(s32[1,3,4,19]{3,2,1,0:T(4,128)S(1)} %constant_dynamic-update-slice_fusion), channel_id=1, source_target_pairs={{4,0},{8,4},{12,8},{5,1},{9,5},{13,9},{6,2},{10,6},{14,10},{7,3},{... | collective-permute-start | bytes 2744 | tf_op jit(solution)/shard_map/ppermute | solution.py:15
  152.2 15.9 %copy-start.6 = (pred[51]{0:T(512)(128)(4,1)S(1)}, pred[51]{0:T(512)(128)(4,1)}, u32[]{:S(2)}) copy-start(pred[51]{0:T(512)(128)(4,1)} %constant.147.clone.1) | copy-start | bytes 157
  152.3 15.9 %copy-start.8 = (s32[1,1,2,50]{3,2,1,0:T(2,128)S(1)}, s32[1,1,2,50]{3,2,1,0:T(2,128)}, u32[]{:S(2)}) copy-start(s32[1,1,2,50]{3,2,1,0:T(2,128)} %param.7) | copy-start | bytes 1204
  168.2 13.8 %copy-start.3 = (bf16[2,19,128,128]{3,2,1,0:T(8,128)(2,1)}, bf16[2,19,128,128]{3,2,1,0:T(8,128)(2,1)S(1)}, u32[]{:S(2)}) copy-start(bf16[2,19,128,128]{3,2,1,0:T(8,128)(2,1)S(1)} %get-tuple-element.292) | copy-start | bytes 3735556 | tf_op jit(solution)/shard_map/while
  209.3 6.8 %copy-start.1 = (f32[51,128,128]{2,1,0:T(8,128)}, f32[51,128,128]{2,1,0:T(8,128)S(1)}, u32[]{:S(2)}) copy-start(f32[51,128,128]{2,1,0:T(8,128)S(1)} %scatter_fusion.1) | copy-start | bytes 10027012 | tf_op jit(solution)/shard_map/while
  273.2 6.2 %copy-start = (f32[51,128,128]{2,1,0:T(8,128)}, f32[51,128,128]{2,1,0:T(8,128)S(1)}, u32[]{:S(2)}) copy-start(f32[51,128,128]{2,1,0:T(8,128)S(1)} %scatter_fusion.2) | copy-start | bytes 10027012 | tf_op jit(solution)/shard_map/while
  296.5 1.8 copy-start.2
  313.4 10.8 %copy-start.4 = (bf16[2,19,128,128]{3,2,1,0:T(8,128)(2,1)S(1)}, bf16[2,19,128,128]{3,2,1,0:T(8,128)(2,1)}, u32[]{:S(2)}) copy-start(bf16[2,19,128,128]{3,2,1,0:T(8,128)(2,1)} %copy-done.3) | copy-start | bytes 3735556 | tf_op jit(solution)/shard_map/while
  324.1 13.8 %copy-start.3 = (bf16[2,19,128,128]{3,2,1,0:T(8,128)(2,1)}, bf16[2,19,128,128]{3,2,1,0:T(8,128)(2,1)S(1)}, u32[]{:S(2)}) copy-start(bf16[2,19,128,128]{3,2,1,0:T(8,128)(2,1)S(1)} %get-tuple-element.292) | copy-start | bytes 3735556 | tf_op jit(solution)/shard_map/while
  365.2 6.8 %copy-start.1 = (f32[51,128,128]{2,1,0:T(8,128)}, f32[51,128,128]{2,1,0:T(8,128)S(1)}, u32[]{:S(2)}) copy-start(f32[51,128,128]{2,1,0:T(8,128)S(1)} %scatter_fusion.1) | copy-start | bytes 10027012 | tf_op jit(solution)/shard_map/while
  429.2 6.2 %copy-start = (f32[51,128,128]{2,1,0:T(8,128)}, f32[51,128,128]{2,1,0:T(8,128)S(1)}, u32[]{:S(2)}) copy-start(f32[51,128,128]{2,1,0:T(8,128)S(1)} %scatter_fusion.2) | copy-start | bytes 10027012 | tf_op jit(solution)/shard_map/while
  452.5 1.8 copy-start.2
  469.4 10.8 %copy-start.4 = (bf16[2,19,128,128]{3,2,1,0:T(8,128)(2,1)S(1)}, bf16[2,19,128,128]{3,2,1,0:T(8,128)(2,1)}, u32[]{:S(2)}) copy-start(bf16[2,19,128,128]{3,2,1,0:T(8,128)(2,1)} %copy-done.3) | copy-start | bytes 3735556 | tf_op jit(solution)/shard_map/while
where the time goes:
time: 485 us; the launch traced here: 480 us
  other arithmetic  146 us (30%)
  waiting for transfers between devices  122 us (25%)
  local copies, waits for them, and re-layouts  117 us (24%)
  matrix products  70 us (14%)
  starting transfers between devices  24.3 us (5%)
    ppermute x4, waiting for transfers between devices, extended(): lax.ppermute(lax.slice_in_dim(block, block.shape[dim] - width, None, axis...  116 us
    scatter-add x8, other arithmetic, one_row(): jax.ops.segment_sum(products.reshape(-1, block_size, block_size), target[...  113 us
    reshape x8, local copies, waits for them, and re-layouts, one_row(): products.reshape(-1, block_size, block_size)  50.7 us
    dot_general x8, matrix products, one_row(): jnp.einsum('kab,kwbc->kwac', own_blocks[start_slot:start_slot + 5], near_...  48.5 us
    gather x2, local copies, waits for them, and re-layouts, one_row(): near_rows = flat_blocks[spots]  26.7 us
    gather x2, local copies, waits for them, and re-layouts, one_row(): padded[chosen]  21.9 us
    dot_general x2, matrix products, one_row(): jnp.einsum('jwab,jwcb->jac', padded[chosen], near_rows, preferred_element...  21.5 us
    concatenate x2, other arithmetic, extended(): block = jnp.concatenate([low, block, high], axis=dim)  15.9 us
  transfers between devices with their start and end apart: 8, of which 4 were waited for; matrix products, arithmetic and copies ran while one was open for 1% of the time, Pallas kernels for 0%

commit v1 on v0

v1 whole, which is shorter than its diff:
```python
import functools

import jax
import jax.numpy as jnp
from jax import lax
from jax.experimental import pallas as pl
from jax.experimental.pallas import tpu as pltpu
from jax.sharding import PartitionSpec as P

PLUS = ((-1, 0), (0, -1), (0, 0), (0, 1), (1, 0))
DIAG = ((-1, -1), (-1, 1), (1, -1), (1, 1))
DEPTH = 4
MESH = pl.DeviceIdType.MESH
NT = (((1,), (1,)), ((), ()))


def ext(a, b):
    return ((a + 2) * 5 + b + 2) * DEPTH


def near(a, b):
    return (a + 1) * 3 + b + 1


def plus_shift(d):
    x = d - 2
    return 2 * x + 2 * x * x * x


def dot(a, b):
    return jnp.dot(a, b, preferred_element_type=jnp.float32)


def dot_nt(a, b):
    return lax.dot_general(a, b, NT, preferred_element_type=jnp.float32)


def kernel(
    rows, cols, slots,
    dens, tab_v, tab_own, mask, place, square_place, live,
    out,
    own, row_lo, row_hi, mid_lo, mid_hi, end_lo, end_hi,
    diag_ll, diag_lh, diag_hl, diag_hh,
    tabs_v, tabs, lhs, acc, square, cubed,
    local_sem, tab_send, tab_recv, tab_local,
    row_send, row_recv, mid_send, mid_recv, end_send, end_recv, diag_send, diag_recv,
):
    r = lax.axis_index("row")
    c = lax.axis_index("col")
    size = own.shape[-1]
    row_bufs, mid_bufs, end_bufs = (row_lo, row_hi), (mid_lo, mid_hi), (end_lo, end_hi)
    diag_bufs = ((diag_ll, diag_lh), (diag_hl, diag_hh))

    def exists(a, b):
        here = None
        for step, at, count in ((a, r, rows), (b, c, cols)):
            test = at > 0 if step < 0 else at < count - 1
            if step:
                here = test if here is None else jnp.logical_and(here, test)
        return here

    def device(a, b):
        return {"row": r + a, "col": c + b}

    around = [s for s in PLUS + DIAG if s != (0, 0)]
    barrier = pltpu.get_barrier_semaphore()
    for a, b in around:
        @pl.when(exists(a, b))
        def _(a=a, b=b):
            pl.semaphore_signal(barrier, inc=1, device_id=device(a, b), device_id_type=MESH)
    high = (r + 1) // rows
    low = (rows - r) // rows
    right = (c + 1) // cols
    left = (cols - c) // cols
    pl.semaphore_wait(barrier, (3 - high - low) * (3 - right - left) - 1)

    def tab_copy(a, b):
        return pltpu.make_async_remote_copy(
            src_ref=tab_v, dst_ref=tabs_v.at[near(-a, -b)],
            send_sem=tab_send.at[near(a, b)], recv_sem=tab_recv.at[near(-a, -b)],
            device_id=device(a, b), device_id_type=MESH)

    def row_copy(side):
        return pltpu.make_async_remote_copy(
            src_ref=dens, dst_ref=row_bufs[side].at[:, pl.ds(0, slots)],
            send_sem=row_send.at[side], recv_sem=row_recv.at[side],
            device_id=device(1 - 2 * side, 0), device_id_type=MESH)

    def mid_copy(side, i):
        return pltpu.make_async_remote_copy(
            src_ref=dens.at[1 + i], dst_ref=mid_bufs[side].at[i, pl.ds(0, slots)],
            send_sem=mid_send.at[side, i], recv_sem=mid_recv.at[side, i],
            device_id=device(0, 1 - 2 * side), device_id_type=MESH)

    def end_copy(side, i):
        return pltpu.make_async_remote_copy(
            src_ref=dens.at[3 * i], dst_ref=end_bufs[side].at[i, pl.ds(0, slots)],
            send_sem=end_send.at[side, i], recv_sem=end_recv.at[side, i],
            device_id=device(0, 1 - 2 * side), device_id_type=MESH)

    def diag_copy(side, col_side, i):
        return pltpu.make_async_remote_copy(
            src_ref=mid_bufs[col_side].at[i, pl.ds(0, slots)],
            dst_ref=diag_bufs[side][col_side].at[i, pl.ds(0, slots)],
            send_sem=diag_send.at[side, col_side, i], recv_sem=diag_recv.at[side, col_side, i],
            device_id=device(1 - 2 * side, 0), device_id_type=MESH)

    sides = (0, 1)
    for a, b in around:
        pl.when(exists(a, b))(lambda a=a, b=b: tab_copy(a, b).start())
    for i in sides:
        for side in sides:
            pl.when(exists(0, 1 - 2 * side))(lambda side=side, i=i: mid_copy(side, i).start())
    for side in sides:
        pl.when(exists(1 - 2 * side, 0))(lambda side=side: row_copy(side).start())
    for i in sides:
        for side in sides:
            pl.when(exists(0, 1 - 2 * side))(lambda side=side, i=i: end_copy(side, i).start())
    load = pltpu.make_async_copy(dens, own.at[:, pl.ds(0, slots)], local_sem)
    load.start()

    blank = jnp.zeros((size, size), own.dtype)
    for buf in (own,) + row_bufs + mid_bufs + end_bufs + diag_bufs[0] + diag_bufs[1]:
        for i in range(buf.shape[0]):
            buf[i, slots] = blank

    @pl.loop(0, acc.shape[0])
    def _(e):
        acc[e] = jnp.zeros((2 * size, size), jnp.float32)

    for a, b in around:
        @pl.when(exists(a, b))
        def _(a=a, b=b):
            tab_copy(-a, -b).wait_recv()
            copy = pltpu.make_async_copy(
                tabs_v.at[near(a, b)], tabs.at[near(a, b)], tab_local.at[near(a, b)])
            copy.start()
            copy.wait()
    load.wait()

    def held(a, b, l, q):
        slot = tab_own[l, q] if (a, b) == (0, 0) else tabs[near(a, b), l, q]
        if (a, b) == (0, 0):
            return own[l, slot]
        if b == 0:
            return row_bufs[(a + 1) // 2][l, slot]
        if a == 0:
            if l in (1, 2):
                return mid_bufs[(b + 1) // 2][l - 1, slot]
            return end_bufs[(b + 1) // 2][l // 3, slot]
        return diag_bufs[(a + 1) // 2][(b + 1) // 2][l - 1, slot]

    planes = range(DEPTH)

    def add_plus(a, b):
        at = PLUS.index((a, b))
        for l in planes:
            for g in (0, 1):
                lhs[g * size:(g + 1) * size, l * size:(l + 1) * size] = own[
                    g + 1, tab_own[g + 1, at * DEPTH + l]]

        @pl.loop(0, len(PLUS))
        def _(d):
            right_side = jnp.concatenate([
                jnp.concatenate([held(a, b, l, d * DEPTH + p) for p in planes], axis=1)
                for l in planes], axis=0)
            total = dot(lhs[...], right_side)
            e = ext(a, b) + plus_shift(d)
            for p in planes:
                acc[e + p] += total[:, p * size:(p + 1) * size]

        for l in planes:
            right_side = jnp.concatenate(
                [held(a, b, l, len(PLUS) * DEPTH + i) for i in range(4)], axis=1)
            total = dot(lhs[:, l * size:(l + 1) * size], right_side)
            for i, (da, db) in enumerate(DIAG):
                acc[ext(a + da, b + db) + l] += total[:, i * size:(i + 1) * size]

    def add_diag(a, b):
        at = len(PLUS) * DEPTH + DIAG.index((a, b))
        for g in (0, 1):
            l = g + 1
            left_side = own[l, tab_own[l, at]]
            half = slice(g * size, (g + 1) * size)

            @pl.loop(0, len(PLUS))
            def _(d):
                right_side = jnp.concatenate(
                    [held(a, b, l, d * DEPTH + p) for p in planes], axis=1)
                total = dot(left_side, right_side)
                e = ext(a, b) + plus_shift(d)
                for p in planes:
                    acc[e + p, half] += total[:, p * size:(p + 1) * size]

            right_side = jnp.concatenate(
                [held(a, b, l, len(PLUS) * DEPTH + i) for i in range(4)], axis=1)
            total = dot(left_side, right_side)
            for i, (da, db) in enumerate(DIAG):
                acc[ext(a + da, b + db) + l, half] += total[:, i * size:(i + 1) * size]

    add_plus(0, 0)
    for i in sides:
        for col_side in sides:
            b = 2 * col_side - 1
            pl.when(exists(0, b))(lambda s=col_side, i=i: mid_copy(s, i).wait_recv())
            for side in sides:
                pl.when(jnp.logical_and(exists(0, b), exists(1 - 2 * side, 0)))(
                    lambda side=side, s=col_side, i=i: diag_copy(side, s, i).start())
    for side in sides:
        a = 2 * side - 1

        @pl.when(exists(a, 0))
        def _(a=a, side=side):
            row_copy(side).wait_recv()
            add_plus(a, 0)
    for side in sides:
        b = 2 * side - 1

        @pl.when(exists(0, b))
        def _(b=b, side=side):
            end_copy(side, 0).wait_recv()
            end_copy(side, 1).wait_recv()
            add_plus(0, b)
    for side in sides:
        for col_side in sides:
            a, b = 2 * side - 1, 2 * col_side - 1

            @pl.when(exists(a, b))
            def _(a=a, b=b, side=side, col_side=col_side):
                diag_copy(side, col_side, 0).wait_recv()
                diag_copy(side, col_side, 1).wait_recv()
                add_diag(a, b)

    @pl.loop(0, acc.shape[0])
    def _(e):
        for g in (0, 1):
            half = slice(g * size, (g + 1) * size)
            square[e, half] = jnp.where(mask[g, e] > 0, acc[e, half], 0.0).astype(square.dtype)

    def cube_plus(a, b):
        first = near(a, b) * DEPTH
        for l in planes:
            left_side = jnp.concatenate(
                [square[ext(a + da, b + db) + l] for da, db in DIAG], axis=1)
            right_side = jnp.concatenate(
                [held(a, b, l, len(PLUS) * DEPTH + i) for i in range(4)], axis=1)
            cubed[first + l] = dot_nt(left_side, right_side)

        @pl.loop(0, len(PLUS))
        def _(d):
            e = ext(a, b) + plus_shift(d)
            left_side = jnp.concatenate([square[e + p] for p in planes], axis=1)
            right_side = jnp.concatenate([
                jnp.concatenate([held(a, b, l, d * DEPTH + p) for p in planes], axis=1)
                for l in planes], axis=0)
            total = dot_nt(left_side, right_side)
            for l in planes:
                cubed[first + l] += total[:, l * size:(l + 1) * size]

    def cube_diag(a, b):
        for g in (0, 1):
            l = g + 1
            half = slice(g * size, (g + 1) * size)
            left_side = jnp.concatenate(
                [square[ext(a + da, b + db) + l, half] for da, db in DIAG]
                + [square[ext(a + da, b + db) + p, half] for da, db in PLUS for p in planes], axis=1)
            places = [len(PLUS) * DEPTH + i for i in range(4)] + list(range(len(PLUS) * DEPTH))
            right_side = jnp.concatenate([held(a, b, l, q) for q in places], axis=1)
            cubed[near(a, b) * DEPTH + l, half] = dot_nt(left_side, right_side)

    cube_plus(0, 0)
    for a, b in around:
        pl.when(exists(a, b))(
            lambda a=a, b=b: cube_diag(a, b) if a and b else cube_plus(a, b))

    @pl.loop(0, slots)
    def _(w):
        for g in (0, 1):
            half = slice(g * size, (g + 1) * size)
            updated = (3.0 * square[square_place[g, w], half].astype(jnp.float32)
                       - 2.0 * cubed[place[g, w], half])
            out[g, w] = jnp.where(live[g, w] > 0, updated, 0.0).astype(out.dtype)

    for a, b in around:
        pl.when(exists(a, b))(lambda a=a, b=b: tab_copy(a, b).wait_send())
    for side in sides:
        pl.when(exists(1 - 2 * side, 0))(lambda side=side: row_copy(side).wait_send())
        for i in sides:
            pl.when(exists(0, 1 - 2 * side))(lambda side=side, i=i: mid_copy(side, i).wait_send())
            pl.when(exists(0, 1 - 2 * side))(lambda side=side, i=i: end_copy(side, i).wait_send())
            for s in sides:
                pl.when(jnp.logical_and(exists(0, 2 * s - 1), exists(1 - 2 * side, 0)))(
                    lambda side=side, s=s, i=i: diag_copy(side, s, i).wait_send())


def shards(rows, cols, density, neighbours, square_pattern):
    density, neighbours, square_pattern = density[0, 0], neighbours[0, 0], square_pattern[0, 0]
    slots, size = density.shape[1], density.shape[2]
    here = (lax.axis_index("row"), lax.axis_index("col"))

    def steps(groups):
        cell = jnp.maximum(groups, 0) // DEPTH
        return cell // cols - here[0], cell % cols - here[1], jnp.maximum(groups, 0) % DEPTH

    da, db, p = steps(neighbours)
    present = neighbours >= 0
    side = 2 + db + 2 * da
    straight = (da * db) == 0
    q = jnp.where(straight, side * DEPTH + p, 20 + (da + 1) + (db + 1) // 2)
    hit = (q[..., None] == jnp.arange(24)) & present[..., None]
    slot_ids = jnp.arange(slots, dtype=jnp.int32)[None, :, None]
    table = slots - jnp.sum(jnp.where(hit, slots - slot_ids, 0), axis=1)
    table = jnp.pad(table.astype(jnp.int32), ((0, 4), (0, 104)), constant_values=slots)
    live = present[1:3].astype(jnp.int32)
    place = jnp.where(present, (near(da, db)) * DEPTH + p, 16)[1:3].astype(jnp.int32)
    square_place = jnp.where(present, ext(da, db) + p, ext(0, 0))[1:3].astype(jnp.int32)
    sa, sb, sp = steps(square_pattern)
    kept = jnp.where(square_pattern >= 0, ext(sa, sb) + sp, -1)
    mask = jnp.any(kept[..., None] == jnp.arange(100), axis=1).astype(jnp.int32)

    block = (size, size)
    dma = pltpu.SemaphoreType.DMA
    bf16 = density.dtype

    def buf(n):
        return pltpu.VMEM((n, slots + 1) + block, bf16)

    smem = pl.BlockSpec(memory_space=pltpu.SMEM)
    purified = pl.pallas_call(
        functools.partial(kernel, rows, cols, slots),
        out_shape=jax.ShapeDtypeStruct((2, slots) + block, bf16),
        in_specs=[pl.BlockSpec(memory_space=pl.ANY), pl.BlockSpec(memory_space=pltpu.VMEM)] + [smem] * 5,
        out_specs=pl.BlockSpec(memory_space=pltpu.VMEM),
        scratch_shapes=[
            buf(4), buf(4), buf(4), buf(2), buf(2), buf(2), buf(2), buf(2), buf(2), buf(2), buf(2),
            pltpu.VMEM((9, 8, 128), jnp.int32),
            pltpu.SMEM((9, 8, 128), jnp.int32),
            pltpu.VMEM((2 * size, DEPTH * size), bf16),
            pltpu.VMEM((100, 2 * size, size), jnp.float32),
            pltpu.VMEM((100, 2 * size, size), bf16),
            pltpu.VMEM((36, 2 * size, size), jnp.float32),
            dma, dma((9,)), dma((9,)), dma((9,)),
            dma((2,)), dma((2,)), dma((2, 2)), dma((2, 2)), dma((2, 2)), dma((2, 2)),
            dma((2, 2, 2)), dma((2, 2, 2)),
        ],
        compiler_params=pltpu.CompilerParams(
            collective_id=0, has_side_effects=True, vmem_limit_bytes=56 * 1024 * 1024),
        cost_estimate=pl.CostEstimate(flops=6 * 10**9, bytes_accessed=20 * 10**6, transcendentals=0),
    )(density, table, table, mask, place, square_place, live)
    return purified[None, None]


def solution(mesh):
    in_specs = (
        P("row", "col", "sys", None, None, None),
        P("row", "col", "sys", None),
        P("row", "col", "sys", None),
    )
    out_specs = P("row", "col", "sys", None, None, None)
    body = functools.partial(shards, mesh.shape["row"], mesh.shape["col"])
    return jax.shard_map(body, mesh=mesh, in_specs=in_specs, out_specs=out_specs, check_vma=False)
```

time: 485 us -> 96.8 us (0.20)
  other arithmetic: 146 us -> 3.55 us
  waiting for transfers between devices: 122 us -> 0 us
  local copies, waits for them, and re-layouts: 117 us -> 4.46 us
  Pallas kernels: 0 us -> 88.5 us
  matrix products: 70 us -> 0 us
  starting transfers between devices: 24.3 us -> 0 us
    ppermute x8 -> x0, waiting for transfers between devices: 122 us -> none  [the longest x4 116 us: extended(): lax.ppermute(lax.slice_in_dim(block, block.shape[dim] - width, None, axis...]
    scatter-add x8 -> x0, other arithmetic: 113 us -> none  [one_row(): jax.ops.segment_sum(products.reshape(-1, block_size, block_size), target[...]
    pallas_call x0 -> x1, Pallas kernels: none -> 88.5 us  [shards(): pl.pallas_call(functools.partial(kernel, rows, cols, slots), out_shape=ja...]
    dot_general x10 -> x0, matrix products: 70 us -> none  [the longest x8 48.5 us: one_row(): jnp.einsum('kab,kwbc->kwac', own_blocks[start_slot:start_slot + 5], near_...]
    reshape x17 -> x0, local copies, waits for them, and re-layouts: 51.4 us -> none  [the longest x8 50.7 us: one_row(): products.reshape(-1, block_size, block_size)]
    gather x8 -> x0, local copies, waits for them, and re-layouts: 51 us -> none  [the longest x2 26.7 us: one_row(): near_rows = flat_blocks[spots]]
    ppermute x8 -> x0, starting transfers between devices: 24.3 us -> none  [the longest x4 14.9 us: extended(): lax.ppermute(lax.slice_in_dim(block, block.shape[dim] - width, None, axis...]
    concatenate x4 -> x0, other arithmetic: 22.7 us -> none  [the longest x2 15.9 us: extended(): block = jnp.concatenate([low, block, high], axis=dim)]
  transfers between devices with their start and end apart: 8 -> 0, of which waited for: 4 -> 0; matrix products, arithmetic and copies ran while one was open for 1% -> 0% of each run, Pallas kernels for 0% -> 0%
where the time goes in v1:
time: 96.8 us; the launch traced here: 96.5 us
  Pallas kernels  88.5 us (91%)
  local copies, waits for them, and re-layouts  4.46 us (5%)
  other arithmetic  3.55 us (4%)
    pallas_call x1, Pallas kernels, shards(): pl.pallas_call(functools.partial(kernel, rows, cols, slots), out_shape=ja...  88.5 us
    unnamed x1, local copies, waits for them, and re-layouts  2.47 us

profile of v1, /device:TPU:11, one launch (start us, length us, event | category | flops | bytes accessed | tf_op | source)
XLA Modules:
  0.0 96.5 jit_solution(481085204457605963)
XLA Ops:
  0.0 0.7 bitcast_select_fusion
  0.7 0.1 fusion
  0.8 0.6 convert_element_type.8.mask
  1.4 0.7 add_select_fusion.5
  2.1 0.6 slice.11.square_place
  2.7 0.6 fusion.16.live
  3.3 0.1 copy.5
  3.4 0.7 add_select_fusion.6
  4.1 0.6 slice.10.place
  4.7 0.1 copy.4
  4.8 0.1 select_reduce_fusion
  5.0 0.6 pad.4.tab_v.tab_own
  5.6 88.5 %shard_map.37 = bf16[2,19,128,128]{3,2,1,0:T(8,128)(2,1)} custom-call(bf16[4,19,128,128]{3,2,1,0:T(8,128)(2,1)} %bitcast.89, s32[8,128]{1,0:T(8,128)} %pad.4.tab_v.tab_own, s32[8,128]{1,0:T(8,128)} %pad.4.tab_v.tab_own, s32[2,100]{1,0:T(2,128)} %convert_element_type.8.mask, s32[2,19]{1,0:T(2,128)} %slice.10.place, s32[2,19]{1,0:T(2,128)} %slice.11.square_place, ...), custom_call_target="tpu_custom_call" | custom-call | flops 6000000000 | bytes 20000000 | tf_op jit(solution)/shard_map/pallas_call | solution.py:329
  94.1 2.5 %copy.7 = bf16[1,1,2,19,128,128]{5,4,3,2,1,0:T(8,128)(2,1)} copy(bf16[1,1,2,19,128,128]{5,4,3,2,1,0:T(8,128)(2,1)} %bitcast.87) | data formatting | bytes 2490368
  (2 shorter events, 0.0 us)

commit v2 on v1

v2 whole, which is shorter than its diff:
```python
import functools

import jax
import jax.numpy as jnp
from jax import lax
from jax.experimental import pallas as pl
from jax.experimental.pallas import tpu as pltpu
from jax.sharding import PartitionSpec as P

PLUS = ((-1, 0), (0, -1), (0, 0), (0, 1), (1, 0))
DIAG = ((-1, -1), (-1, 1), (1, -1), (1, 1))
DEPTH = 4
UNROLL = True
MESH = pl.DeviceIdType.MESH
NT = (((1,), (1,)), ((), ()))


def ext(a, b):
    return ((a + 2) * 5 + b + 2) * DEPTH


def near(a, b):
    return (a + 1) * 3 + b + 1


def plus_shift(d):
    x = d - 2
    return 2 * x + 2 * x * x * x


def dot(a, b):
    return jnp.dot(a, b, preferred_element_type=jnp.float32)


def dot_nt(a, b):
    return lax.dot_general(a, b, NT, preferred_element_type=jnp.float32)


def kernel(
    rows, cols, slots,
    dens, nbrs, pattern,
    out,
    own, row_lo, row_hi, mid_lo, mid_hi, end_lo0, end_lo3, end_hi0, end_hi3,
    diag_ll1, diag_ll2, diag_lh1, diag_lh2, diag_hl1, diag_hl2, diag_hh1, diag_hh2,
    meta_v, meta, lists, tabs_v, tabs, lhs, acc, square, cubed,
    local_sem, meta_sem, tab_send, tab_recv, tab_local,
    row_send, row_recv, mid_send, mid_recv, end_send, end_recv, diag_send, diag_recv,
):
    r = lax.axis_index("row")
    c = lax.axis_index("col")
    size = own.shape[-1]
    row_bufs, mid_bufs, end_bufs = (row_lo, row_hi), (mid_lo, mid_hi), ((end_lo0, end_lo3), (end_hi0, end_hi3))
    diag_bufs = (((diag_ll1, diag_ll2), (diag_lh1, diag_lh2)), ((diag_hl1, diag_hl2), (diag_hh1, diag_hh2)))

    def exists(a, b):
        here = None
        for step, at, count in ((a, r, rows), (b, c, cols)):
            test = at > 0 if step < 0 else at < count - 1
            if step:
                here = test if here is None else jnp.logical_and(here, test)
        return here

    def device(a, b):
        return {"row": r + a, "col": c + b}

    around = [s for s in PLUS + DIAG if s != (0, 0)]
    barrier = pltpu.get_barrier_semaphore()
    for a, b in around:
        @pl.when(exists(a, b))
        def _(a=a, b=b):
            pl.semaphore_signal(barrier, inc=1, device_id=device(a, b), device_id_type=MESH)
    high = (r + 1) // rows
    low = (rows - r) // rows
    right = (c + 1) // cols
    left = (cols - c) // cols
    pl.semaphore_wait(barrier, (3 - high - low) * (3 - right - left) - 1)

    def tab_copy(a, b):
        return pltpu.make_async_remote_copy(
            src_ref=lists.at[4], dst_ref=lists.at[near(-a, -b)],
            send_sem=tab_send.at[near(a, b)], recv_sem=tab_recv.at[near(-a, -b)],
            device_id=device(a, b), device_id_type=MESH)

    def row_copy(side):
        return pltpu.make_async_remote_copy(
            src_ref=dens, dst_ref=row_bufs[side].at[:, pl.ds(0, slots)],
            send_sem=row_send.at[side], recv_sem=row_recv.at[side],
            device_id=device(1 - 2 * side, 0), device_id_type=MESH)

    def mid_copy(side, i):
        return pltpu.make_async_remote_copy(
            src_ref=dens.at[1 + i], dst_ref=mid_bufs[side].at[i, pl.ds(0, slots)],
            send_sem=mid_send.at[side, i], recv_sem=mid_recv.at[side, i],
            device_id=device(0, 1 - 2 * side), device_id_type=MESH)

    def end_copy(side, i):
        return pltpu.make_async_remote_copy(
            src_ref=dens.at[3 * i], dst_ref=end_bufs[side][i].at[0, pl.ds(0, slots)],
            send_sem=end_send.at[side, i], recv_sem=end_recv.at[side, i],
            device_id=device(0, 1 - 2 * side), device_id_type=MESH)

    def diag_copy(side, col_side, i):
        return pltpu.make_async_remote_copy(
            src_ref=mid_bufs[col_side].at[i, pl.ds(0, slots)],
            dst_ref=diag_bufs[side][col_side][i].at[0, pl.ds(0, slots)],
            send_sem=diag_send.at[side, col_side, i], recv_sem=diag_recv.at[side, col_side, i],
            device_id=device(1 - 2 * side, 0), device_id_type=MESH)

    sides = (0, 1)
    lists[4] = jnp.zeros_like(lists[4])
    lists[4, 0:DEPTH, 0:slots] = nbrs[...]
    for a, b in around:
        pl.when(exists(a, b))(lambda a=a, b=b: tab_copy(a, b).start())
    for i in sides:
        for side in sides:
            pl.when(exists(0, 1 - 2 * side))(lambda side=side, i=i: mid_copy(side, i).start())
    for side in sides:
        pl.when(exists(1 - 2 * side, 0))(lambda side=side: row_copy(side).start())
    for i in sides:
        for side in sides:
            pl.when(exists(0, 1 - 2 * side))(lambda side=side, i=i: end_copy(side, i).start())
    load = pltpu.make_async_copy(dens, own.at[:, pl.ds(0, slots)], local_sem)
    load.start()

    def steps(groups):
        known = jnp.maximum(groups, 0)
        cell = jnp.right_shift(known, DEPTH.bit_length() - 1)
        row = jnp.zeros_like(cell)
        for i in range(1, rows):
            row += (cell >= i * cols).astype(jnp.int32)
        return row, cell - row * cols, jnp.bitwise_and(known, DEPTH - 1)

    lanes = lax.broadcasted_iota(jnp.int32, (1, meta_v.shape[2]), 1)

    def slot_table(listed, a, b):
        row, col, p = steps(listed)
        da, db = row - r - a, col - c - b
        corner = 20 + (da + 1) + jnp.right_shift(db + 1, 1)
        q = jnp.where(da * db == 0, (2 + db + 2 * da) * DEPTH + p, corner)
        q = jnp.where(listed >= 0, q, -1)
        table = jnp.full((DEPTH, meta_v.shape[2]), slots, jnp.int32)
        for w in range(slots):
            table = jnp.where(lanes == q[:, w:w + 1], w, table)
        return table, da, db, p

    meta_v[...] = jnp.zeros_like(meta_v)
    tabs_v[...] = jnp.zeros_like(tabs_v)
    listed = nbrs[...]
    present = listed >= 0
    table, da, db, p = slot_table(listed, 0, 0)
    meta_v[0, 0:DEPTH] = table
    meta_v[2, 0:DEPTH, 0:slots] = jnp.clip(
        jnp.where(present, near(da, db) * DEPTH + p, 16), 0, cubed.shape[0] - 1)
    meta_v[3, 0:DEPTH, 0:slots] = jnp.clip(
        jnp.where(present, ext(da, db) + p, ext(0, 0)), 0, square.shape[0] - 1)
    meta_v[4, 0:DEPTH, 0:slots] = present.astype(jnp.int32)
    listed = pattern[...]
    row, col, p = steps(listed)
    kept = jnp.where(listed >= 0, ext(row - r, col - c) + p, -1)
    mask = jnp.zeros((2, meta_v.shape[2]), jnp.int32)
    for i in range(listed.shape[1]):
        mask = jnp.where(lanes == kept[:, i:i + 1], 1, mask)
    meta_v[1, 0:2] = mask
    meta_load = pltpu.make_async_copy(meta_v, meta, meta_sem)
    meta_load.start()
    meta_load.wait()

    blank = jnp.zeros((size, size), own.dtype)
    single = end_bufs + diag_bufs[0] + diag_bufs[1]
    for buf in (own,) + row_bufs + mid_bufs + tuple(b for pair in single for b in pair):
        for i in range(buf.shape[0]):
            buf[i, slots] = blank

    @pl.loop(0, acc.shape[0])
    def _(e):
        acc[e] = jnp.zeros((2 * size, size), jnp.float32)

    for a, b in around:
        @pl.when(exists(a, b))
        def _(a=a, b=b):
            tab_copy(-a, -b).wait_recv()
            tabs_v[near(a, b), 0:DEPTH] = slot_table(lists[near(a, b), 0:DEPTH, 0:slots], a, b)[0]
            copy = pltpu.make_async_copy(
                tabs_v.at[near(a, b)], tabs.at[near(a, b)], tab_local.at[near(a, b)])
            copy.start()
            copy.wait()
    load.wait()

    def held(a, b, l, q):
        slot = meta[0, l, q] if (a, b) == (0, 0) else tabs[near(a, b), l, q]
        if (a, b) == (0, 0):
            return own[l, slot]
        if b == 0:
            return row_bufs[(a + 1) // 2][l, slot]
        if a == 0:
            if l in (1, 2):
                return mid_bufs[(b + 1) // 2][l - 1, slot]
            return end_bufs[(b + 1) // 2][l // 3][0, slot]
        return diag_bufs[(a + 1) // 2][(b + 1) // 2][l - 1][0, slot]

    planes = range(DEPTH)

    def add_plus(a, b, some):
        at = PLUS.index((a, b))
        for i, l in enumerate(some):
            for g in (0, 1):
                lhs[g * size:(g + 1) * size, i * size:(i + 1) * size] = own[
                    g + 1, meta[0, g + 1, at * DEPTH + l]]

        @pl.loop(0, len(PLUS), unroll=UNROLL)
        def _(d):
            right_side = jnp.concatenate([
                jnp.concatenate([held(a, b, l, d * DEPTH + p) for p in planes], axis=1)
                for l in some], axis=0)
            total = dot(lhs[:, :len(some) * size], right_side)
            e = ext(a, b) + plus_shift(d)
            for p in planes:
                acc[e + p] += total[:, p * size:(p + 1) * size]

        for j, l in enumerate(some):
            right_side = jnp.concatenate(
                [held(a, b, l, len(PLUS) * DEPTH + i) for i in range(4)], axis=1)
            total = dot(lhs[:, j * size:(j + 1) * size], right_side)
            for i, (da, db) in enumerate(DIAG):
                acc[ext(a + da, b + db) + l] += total[:, i * size:(i + 1) * size]

    def add_diag(a, b, g):
        at = len(PLUS) * DEPTH + DIAG.index((a, b))
        l = g + 1
        left_side = own[l, meta[0, l, at]]
        half = slice(g * size, (g + 1) * size)

        @pl.loop(0, len(PLUS), unroll=UNROLL)
        def _(d):
            right_side = jnp.concatenate(
                [held(a, b, l, d * DEPTH + p) for p in planes], axis=1)
            total = dot(left_side, right_side)
            e = ext(a, b) + plus_shift(d)
            for p in planes:
                acc[e + p, half] += total[:, p * size:(p + 1) * size]

        right_side = jnp.concatenate(
            [held(a, b, l, len(PLUS) * DEPTH + i) for i in range(4)], axis=1)
        total = dot(left_side, right_side)
        for i, (da, db) in enumerate(DIAG):
            acc[ext(a + da, b + db) + l, half] += total[:, i * size:(i + 1) * size]

    def forward(i):
        for col_side in sides:
            b = 2 * col_side - 1
            pl.when(exists(0, b))(lambda s=col_side: mid_copy(s, i).wait_recv())
            for side in sides:
                pl.when(jnp.logical_and(exists(0, b), exists(1 - 2 * side, 0)))(
                    lambda side=side, s=col_side: diag_copy(side, s, i).start())

    def finish(first, count):
        @pl.loop(0, count, unroll=1 if count % 2 else 2)
        def _(i):
            e = first + i
            for g in (0, 1):
                half = slice(g * size, (g + 1) * size)
                square[e, half] = jnp.where(meta[1, g, e] > 0, acc[e, half], 0.0).astype(square.dtype)

    add_plus(0, 0, planes)
    forward(0)
    forward(1)
    for side in sides:
        a = 2 * side - 1

        @pl.when(exists(a, 0))
        def _(a=a, side=side):
            row_copy(side).wait_recv()
            add_plus(a, 0, planes)
    for side in sides:
        b = 2 * side - 1
        pl.when(exists(0, b))(lambda b=b: add_plus(0, b, (1, 2)))

    def end_part(i):
        for side in sides:
            b = 2 * side - 1

            @pl.when(exists(0, b))
            def _(b=b, side=side):
                end_copy(side, i).wait_recv()
                add_plus(0, b, (3 * i,))

    def diag_part(i):
        for side in sides:
            for col_side in sides:
                a, b = 2 * side - 1, 2 * col_side - 1

                @pl.when(exists(a, b))
                def _(a=a, b=b, side=side, col_side=col_side):
                    diag_copy(side, col_side, i).wait_recv()
                    add_diag(a, b, i)

    diag_part(0)
    end_part(0)
    diag_part(1)
    for a in (-2, 2):
        finish(ext(a, -1), 3 * DEPTH)
        for b in (-2, 2):
            finish(ext(a, b) + 1, 2)
    for a in (-1, 1):
        for b in (-2, 0, 2):
            finish(ext(a, b), 3)
    end_part(1)
    finish(ext(0, -2), 5 * DEPTH)
    for a in (-1, 1):
        for b in (-2, 0, 2):
            finish(ext(a, b) + 3, 1)
        for b in (-1, 1):
            finish(ext(a, b), DEPTH)

    def cube_plus(a, b):
        first = near(a, b) * DEPTH
        for l in planes:
            left_side = jnp.concatenate(
                [square[ext(a + da, b + db) + l] for da, db in DIAG], axis=1)
            right_side = jnp.concatenate(
                [held(a, b, l, len(PLUS) * DEPTH + i) for i in range(4)], axis=1)
            cubed[first + l] = dot_nt(left_side, right_side)

        @pl.loop(0, len(PLUS), unroll=UNROLL)
        def _(d):
            e = ext(a, b) + plus_shift(d)
            left_side = jnp.concatenate([square[e + p] for p in planes], axis=1)
            right_side = jnp.concatenate([
                jnp.concatenate([held(a, b, l, d * DEPTH + p) for p in planes], axis=1)
                for l in planes], axis=0)
            total = dot_nt(left_side, right_side)
            for l in planes:
                cubed[first + l] += total[:, l * size:(l + 1) * size]

    def cube_diag(a, b):
        for g in (0, 1):
            l = g + 1
            half = slice(g * size, (g + 1) * size)
            left_side = jnp.concatenate(
                [square[ext(a + da, b + db) + l, half] for da, db in DIAG]
                + [square[ext(a + da, b + db) + p, half] for da, db in PLUS for p in planes], axis=1)
            places = [len(PLUS) * DEPTH + i for i in range(4)] + list(range(len(PLUS) * DEPTH))
            right_side = jnp.concatenate([held(a, b, l, q) for q in places], axis=1)
            cubed[near(a, b) * DEPTH + l, half] = dot_nt(left_side, right_side)

    cube_plus(0, 0)
    for a, b in around:
        pl.when(exists(a, b))(
            lambda a=a, b=b: cube_diag(a, b) if a and b else cube_plus(a, b))

    @pl.loop(0, slots, unroll=1)
    def _(w):
        for g in (0, 1):
            half = slice(g * size, (g + 1) * size)
            updated = (3.0 * square[meta[3, g + 1, w], half].astype(jnp.float32)
                       - 2.0 * cubed[meta[2, g + 1, w], half])
            out[g, w] = jnp.where(meta[4, g + 1, w] > 0, updated, 0.0).astype(out.dtype)

    for a, b in around:
        pl.when(exists(a, b))(lambda a=a, b=b: tab_copy(a, b).wait_send())
    for side in sides:
        pl.when(exists(1 - 2 * side, 0))(lambda side=side: row_copy(side).wait_send())
        for i in sides:
            pl.when(exists(0, 1 - 2 * side))(lambda side=side, i=i: mid_copy(side, i).wait_send())
            pl.when(exists(0, 1 - 2 * side))(lambda side=side, i=i: end_copy(side, i).wait_send())
            for s in sides:
                pl.when(jnp.logical_and(exists(0, 2 * s - 1), exists(1 - 2 * side, 0)))(
                    lambda side=side, s=s, i=i: diag_copy(side, s, i).wait_send())


def shards(rows, cols, density, neighbours, square_pattern):
    density, neighbours, square_pattern = density[0, 0], neighbours[0, 0], square_pattern[0, 0]
    slots, size = density.shape[1], density.shape[2]
    block = (size, size)
    dma = pltpu.SemaphoreType.DMA
    bf16 = density.dtype

    def buf(n):
        return pltpu.VMEM((n, slots + 1) + block, bf16)

    purified = pl.pallas_call(
        functools.partial(kernel, rows, cols, slots),
        out_shape=jax.ShapeDtypeStruct((2, slots) + block, bf16),
        in_specs=[pl.BlockSpec(memory_space=pl.ANY)] + [pl.BlockSpec(memory_space=pltpu.VMEM)] * 2,
        out_specs=pl.BlockSpec(memory_space=pltpu.VMEM),
        scratch_shapes=[
            buf(4), buf(4), buf(4), buf(2), buf(2),
            *[buf(1)] * 12,
            pltpu.VMEM((5, 8, 128), jnp.int32),
            pltpu.SMEM((5, 8, 128), jnp.int32),
            pltpu.VMEM((9, 8, 128), jnp.int32),
            pltpu.VMEM((9, 8, 128), jnp.int32),
            pltpu.SMEM((9, 8, 128), jnp.int32),
            pltpu.VMEM((2 * size, DEPTH * size), bf16),
            pltpu.VMEM((100, 2 * size, size), jnp.float32),
            pltpu.VMEM((100, 2 * size, size), bf16),
            pltpu.VMEM((36, 2 * size, size), jnp.float32),
            dma, dma, dma((9,)), dma((9,)), dma((9,)),
            dma((2,)), dma((2,)), dma((2, 2)), dma((2, 2)), dma((2, 2)), dma((2, 2)),
            dma((2, 2, 2)), dma((2, 2, 2)),
        ],
        compiler_params=pltpu.CompilerParams(
            collective_id=0, has_side_effects=True, vmem_limit_bytes=56 * 1024 * 1024),
        cost_estimate=pl.CostEstimate(flops=6 * 10**9, bytes_accessed=20 * 10**6, transcendentals=0),
    )(density, neighbours, square_pattern)
    return purified[None, None]


def solution(mesh):
    in_specs = (
        P("row", "col", "sys", None, None, None),
        P("row", "col", "sys", None),
        P("row", "col", "sys", None),
    )
    out_specs = P("row", "col", "sys", None, None, None)
    body = functools.partial(shards, mesh.shape["row"], mesh.shape["col"])
    return jax.shard_map(body, mesh=mesh, in_specs=in_specs, out_specs=out_specs, check_vma=False)
```

time: 96.8 us -> 75.1 us (0.78)
  Pallas kernels: 88.5 us -> 72.5 us
  other arithmetic: 3.55 us -> 0 us
  local copies, waits for them, and re-layouts: 4.46 us -> 2.47 us
    pallas_call x1, Pallas kernels: 88.5 us -> 72.5 us  [shards(): pl.pallas_call(functools.partial(kernel, rows, cols, slots), out_shape=ja...]
    select_n x3 -> x0, other arithmetic: 2.11 us -> none  [the longest x1 0.71 us: shards(): jnp.where(present, near(da, db) * DEPTH + p, 16)[1:3].astype(jnp.int32)]
    convert_element_type x2 -> x0, other arithmetic: 1.2 us -> none  [the longest x1 0.6 us: shards(): mask = jnp.any(kept[..., None] == jnp.arange(100), axis=1).astype(jnp.int32)]
    slice x2 -> x0, local copies, waits for them, and re-layouts: 1.18 us -> none  [the longest x1 0.59 us: shards(): jnp.where(present, ext(da, db) + p, ext(0, 0))[1:3].astype(jnp.int32)]
where the time goes in v2:
time: 75.1 us; the launch traced here: 75 us
  Pallas kernels  72.5 us (97%)
  local copies, waits for them, and re-layouts  2.47 us (3%)
    pallas_call x1, Pallas kernels, shards(): pl.pallas_call(functools.partial(kernel, rows, cols, slots), out_shape=ja...  72.5 us
    unnamed x1, local copies, waits for them, and re-layouts  2.47 us

profile of v2, /device:TPU:11, one launch (start us, length us, event | category | flops | bytes accessed | tf_op | source)
XLA Modules:
  0.0 75.0 jit_solution(17357607432003389631)
XLA Ops:
  0.0 72.5 %shard_map.37 = bf16[2,19,128,128]{3,2,1,0:T(8,128)(2,1)} custom-call(bf16[4,19,128,128]{3,2,1,0:T(8,128)(2,1)} %bitcast.5, s32[4,19]{1,0:T(4,128)} %bitcast.6, s32[2,50]{1,0:T(2,128)} %bitcast.7), custom_call_target="tpu_custom_call" | custom-call | flops 6000000000 | bytes 20000000 | tf_op jit(solution)/shard_map/pallas_call | solution.py:381
  72.5 2.5 %copy.5 = bf16[1,1,2,19,128,128]{5,4,3,2,1,0:T(8,128)(2,1)} copy(bf16[1,1,2,19,128,128]{5,4,3,2,1,0:T(8,128)(2,1)} %bitcast.4) | data formatting | bytes 2490368

commit v3 on v2

--- a/solution.py
+++ b/solution.py
@@ -254,7 +254,7 @@
                     lambda side=side, s=col_side: diag_copy(side, s, i).start())
 
     def finish(first, count):
-        @pl.loop(0, count, unroll=1 if count % 2 else 2)
+        @pl.loop(0, count, unroll=1 if count % 4 else 4)
         def _(i):
             e = first + i
             for g in (0, 1):
@@ -348,7 +348,7 @@
         pl.when(exists(a, b))(
             lambda a=a, b=b: cube_diag(a, b) if a and b else cube_plus(a, b))
 
-    @pl.loop(0, slots, unroll=1)
+    @pl.loop(0, slots, unroll=True)
     def _(w):
         for g in (0, 1):
             half = slice(g * size, (g + 1) * size)

time: 75.1 us -> 74.8 us (level)
  no operation moved by 1% of the time
where the time goes in v3:
time: 74.8 us; the launch traced here: 74.7 us
  Pallas kernels  72.2 us (97%)
  local copies, waits for them, and re-layouts  2.47 us (3%)
    pallas_call x1, Pallas kernels, shards(): pl.pallas_call(functools.partial(kernel, rows, cols, slots), out_shape=ja...  72.2 us
    unnamed x1, local copies, waits for them, and re-layouts  2.47 us

profile of v3, /device:TPU:11, one launch (start us, length us, event | category | flops | bytes accessed | tf_op | source)
XLA Modules:
  0.0 74.7 jit_solution(16762443122935608349)
XLA Ops:
  0.0 72.2 %shard_map.37 = bf16[2,19,128,128]{3,2,1,0:T(8,128)(2,1)} custom-call(bf16[4,19,128,128]{3,2,1,0:T(8,128)(2,1)} %bitcast.5, s32[4,19]{1,0:T(4,128)} %bitcast.6, s32[2,50]{1,0:T(2,128)} %bitcast.7), custom_call_target="tpu_custom_call" | custom-call | flops 6000000000 | bytes 20000000 | tf_op jit(solution)/shard_map/pallas_call | solution.py:381
  72.2 2.5 %copy.5 = bf16[1,1,2,19,128,128]{5,4,3,2,1,0:T(8,128)(2,1)} copy(bf16[1,1,2,19,128,128]{5,4,3,2,1,0:T(8,128)(2,1)} %bitcast.4) | data formatting | bytes 2490368
